TPU v7x, 32 devices: a whole 2x2x4 slice. The times are simulated.
32 devices in a mesh: group: 2 (over x), ctx: 16 (over z, y, core).
Axes of the slice: x: 2, y: 2, z: 4, core: 2. Of those that a mesh axis runs over, the one named last changes fastest.
Arguments:
- hyena_qkv: bfloat16 [4096, 3, 2048], P(('group', 'ctx')), parts along dimension 0, may hold values from -6 to 6
- short_weight: float32 [3, 3, 2048], replicated, may hold values from -3.5 to 3.5
- filter_rate: float32 [128, 16], replicated, as said below
- filter_residue: float32 [128, 16], replicated, may hold values from -4 to 4
- attn_qkv: bfloat16 [4096, 3, 2048], P(('group', 'ctx')), parts along dimension 0, may hold values from -6 to 6
- doc_lengths: int32 [8], P('group'), parts along dimension 0, may hold values from 1 to 897, 2048 in all
Outputs:
- hyena_out: bfloat16 [4096, 2048], P(('group', 'ctx')), parts along dimension 0
- attn_out: bfloat16 [4096, 2048], P(('group', 'ctx')), parts along dimension 0
There are 2 independent parts, one for each index of `group`. A program takes and returns all parts, laid end to end along the dimension named above; an argument that names none is the same for every part. Nothing has to cross between parts.
Inputs may be any that keep to these rules, and one draw needn't show every extreme that they name: `filter_rate`: every rate is positive and at most 1/30. `doc_lengths`: the lengths sum to 2048 and the longest is exactly 897.
All inputs are finite; a program needn't handle non-finite values.
Results may differ from a plain program's by a relative error of at most 0.0054.
Values may be sent and summed in bfloat16 or wider, within the bound.
A program may use at most 128 MiB of HBM per device.

v0:
```python
import math

import jax
import jax.numpy as jnp
from jax import lax
from jax.sharding import PartitionSpec as P

HEAD = 128
SPAN = 8


precise = lax.Precision.HIGHEST


def from_behind(value, axis, steps):
    count = lax.axis_size(axis)
    initial, last = (max(0, -steps), min(count, count - steps))
    return lax.ppermute(value, axis, [(source, source + steps) for source in range(initial, last)])


def featurize(token_rows, before, short_weight):
    row_count = token_rows.shape[0]
    padded = jnp.concatenate([before, token_rows], axis=0).astype(jnp.float32)
    return (
        short_weight[0] * padded[2:]
        + short_weight[1] * padded[1 : row_count + 1]
        + short_weight[2] * padded[:row_count]
    )


def filter_terms(filter_rate, filter_residue, row_count):
    mode_coeff = filter_residue * jnp.sqrt(2.0 * filter_rate / filter_rate.shape[1])
    lag_values = jnp.arange(row_count).astype(jnp.float32)
    powers = jnp.exp(-filter_rate[:, :, None] * lag_values)
    filter_taps = jnp.einsum("gm,gmk->gk", mode_coeff, powers, precision=precise)
    return (mode_coeff, filter_taps.astype(jnp.bfloat16))


def toeplitz(filter_taps):
    row_count = filter_taps.shape[1]
    lag_index = (
        jnp.arange(row_count, dtype=jnp.int32)[:, None]
        - jnp.arange(row_count, dtype=jnp.int32)[None, :]
    )
    lag_table = jnp.take(filter_taps, jnp.clip(lag_index, 0, row_count - 1), axis=1)
    return jnp.where(lag_index[None] >= 0, lag_table, jnp.zeros((), filter_taps.dtype))


def block_ends(mixed_in, filter_rate):
    row_count, channels = mixed_in.shape
    groups = filter_rate.shape[0]
    lag_values = (row_count - 1 - jnp.arange(row_count)).astype(jnp.float32)
    powers = jnp.exp(-filter_rate[:, :, None] * lag_values)
    grouped = mixed_in.astype(jnp.float32).reshape(row_count, groups, channels // groups)
    return jnp.einsum("gms,sgc->gmc", powers, grouped, precision=precise)


def block_far(carried, filter_rate, mode_coeff, row_count):
    lag_values = jnp.arange(1, row_count + 1).astype(jnp.float32)
    powers = mode_coeff[:, :, None] * jnp.exp(-filter_rate[:, :, None] * lag_values)
    return jnp.einsum("gmt,gmc->tgc", powers, carried, precision=precise)


def visible(query_pos, key_pos, doc_lengths):
    bounds = jnp.cumsum(doc_lengths, dtype=jnp.int32)
    query_doc = jnp.sum((query_pos[:, None] >= bounds[None, :]).astype(jnp.int32), axis=1)
    key_doc = jnp.sum((key_pos[:, None] >= bounds[None, :]).astype(jnp.int32), axis=1)
    causal = (key_pos[None, :] <= query_pos[:, None]) & (key_pos[None, :] >= 0)
    return causal & (key_doc[None, :] == query_doc[:, None])


def attend(queries, keys, values, allowed):
    row_count, channels = queries.shape
    heads = channels // HEAD

    def split_heads(matrix):
        return matrix.reshape(matrix.shape[0], heads, HEAD).transpose(1, 0, 2)

    def one_head(head_parts):
        query_rows, key_rows, value_rows = head_parts
        scores = jnp.dot(query_rows, key_rows.T, preferred_element_type=jnp.float32) * (
            1.0 / math.sqrt(HEAD)
        )
        scores = jnp.where(allowed, scores, -jnp.inf)
        row_max = jnp.max(scores, axis=1, keepdims=True)
        exp_scores = jnp.exp(scores - row_max)
        weight = (exp_scores / jnp.sum(exp_scores, axis=1, keepdims=True)).astype(jnp.bfloat16)
        return jnp.dot(weight, value_rows, preferred_element_type=jnp.float32).astype(jnp.bfloat16)

    head_out = lax.map(one_head, (split_heads(queries), split_heads(keys), split_heads(values)))
    return head_out.transpose(1, 0, 2).reshape(row_count, channels)


def on_device(hyena_qkv, short_weight, filter_rate, filter_residue, attn_qkv, doc_lengths):
    row_count = hyena_qkv.shape[0]
    channels = hyena_qkv.shape[2]
    groups = filter_rate.shape[0]
    device_index = lax.axis_index("ctx")
    before = from_behind(hyena_qkv[row_count - 2 :], "ctx", 1)
    featured = featurize(hyena_qkv, before, short_weight)
    mixed_in = (featured[:, 1] * featured[:, 2]).astype(jnp.bfloat16)
    mode_coeff, filter_taps = filter_terms(filter_rate, filter_residue, row_count)
    grouped = mixed_in.reshape(row_count, groups, channels // groups)
    near_part = jnp.einsum(
        "gts,sgc->tgc", toeplitz(filter_taps), grouped, preferred_element_type=jnp.float32
    )
    end_states = block_ends(mixed_in, filter_rate)
    pieces = lax.all_gather(end_states[None], "ctx", axis=0, tiled=True)
    owners = jnp.arange(pieces.shape[0], dtype=jnp.int32)
    absorb_distance = device_index - 1 - owners
    lag_values = (jnp.maximum(absorb_distance, 0) * row_count).astype(jnp.float32)
    powers = jnp.exp(-filter_rate[None] * lag_values[:, None, None])
    powers = jnp.where((absorb_distance >= 0)[:, None, None], powers, 0.0)
    carried = jnp.einsum("ngm,ngmc->gmc", powers, pieces, precision=precise)
    far_part = block_far(carried, filter_rate, mode_coeff, row_count)
    hyena_out = (featured[:, 0] * (near_part + far_part).reshape(row_count, channels)).astype(
        jnp.bfloat16
    )
    key_pairs = attn_qkv[:, 1:]
    key_blocks = [key_pairs]
    moving = key_pairs
    for distance in range(1, SPAN):
        moving = from_behind(moving, "ctx", 1)
        key_blocks.append(moving)
    window = jnp.concatenate(key_blocks[::-1], axis=0)
    query_pos = device_index * row_count + jnp.arange(row_count, dtype=jnp.int32)
    key_pos = (device_index - SPAN + 1) * row_count + jnp.arange(SPAN * row_count, dtype=jnp.int32)
    allowed = visible(query_pos, key_pos, doc_lengths)
    attn_out = attend(attn_qkv[:, 0], window[:, 0], window[:, 1], allowed)
    return (hyena_out, attn_out)


def solution(mesh):
    in_specs = (
        P(("group", "ctx"), None, None),
        P(),
        P(),
        P(),
        P(("group", "ctx"), None, None),
        P("group"),
    )
    out_specs = (P(("group", "ctx"), None), P(("group", "ctx"), None))
    return jax.shard_map(
        on_device, mesh=mesh, in_specs=in_specs, out_specs=out_specs, check_vma=False
    )
```

profile of v0, /device:TPU:13, one launch (start us, length us, event | category | flops | bytes accessed | tf_op | source)
XLA Modules:
  0.0 266.5 jit_solution(11131418573891220046)
XLA Ops:
  7.2 1.3 slice.53
  9.2 3.7 %collective-permute-start.1 = (bf16[128,2,2048]{0,2,1:T(8,128)(2,1)S(1)}, bf16[128,2,2048]{0,2,1:T(8,128)(2,1)}, u32[]{:S(2)}, u32[]{:S(2)}) collective-permute-start(bf16[128,2,2048]{0,2,1:T(8,128)(2,1)S(1)} %copy.73), channel_id=1, source_target_pairs={{0,1},{1,2},{2,3},{3,4},{4,5},{5,6},{6,7},{7,8},{8,9},{9,10},{10,1... | collective-permute-start | bytes 3145736 | tf_op jit(solution)/shard_map/ppermute | solution.py:18
  13.9 1.9 collective-permute-start
  15.8 8.9 %collective-permute-done.1 = bf16[128,2,2048]{0,2,1:T(8,128)(2,1)} collective-permute-done((bf16[128,2,2048]{0,2,1:T(8,128)(2,1)S(1)}, bf16[128,2,2048]{0,2,1:T(8,128)(2,1)}, u32[]{:S(2)}, u32[]{:S(2)}) %collective-permute-start.1) | collective-permute-done | bytes 1048608 | tf_op jit(solution)/shard_map/ppermute | solution.py:18
  24.7 5.4 %collective-permute-start.2 = (bf16[128,2,2048]{0,2,1:T(8,128)(2,1)}, bf16[128,2,2048]{0,2,1:T(8,128)(2,1)}, u32[]{:S(2)}, u32[]{:S(2)}) collective-permute-start(bf16[128,2,2048]{0,2,1:T(8,128)(2,1)} %collective-permute-done.1), channel_id=1, source_target_pairs={{0,1},{1,2},{2,3},{3,4},{4,5},{5,6},{6,7},{7,8},{8,9},{9,10},{10,1... | collective-permute-start | bytes 3145736 | tf_op jit(solution)/shard_map/ppermute | solution.py:18
  30.1 1.9 copy.44
  34.2 7.9 %collective-permute-done.2 = bf16[128,2,2048]{0,2,1:T(8,128)(2,1)} collective-permute-done((bf16[128,2,2048]{0,2,1:T(8,128)(2,1)}, bf16[128,2,2048]{0,2,1:T(8,128)(2,1)}, u32[]{:S(2)}, u32[]{:S(2)}) %collective-permute-start.2) | collective-permute-done | bytes 1048608 | tf_op jit(solution)/shard_map/ppermute | solution.py:18
  42.1 5.3 %collective-permute-start.3 = (bf16[128,2,2048]{0,2,1:T(8,128)(2,1)}, bf16[128,2,2048]{0,2,1:T(8,128)(2,1)}, u32[]{:S(2)}, u32[]{:S(2)}) collective-permute-start(bf16[128,2,2048]{0,2,1:T(8,128)(2,1)} %collective-permute-done.2), channel_id=1, source_target_pairs={{0,1},{1,2},{2,3},{3,4},{4,5},{5,6},{6,7},{7,8},{8,9},{9,10},{10,1... | collective-permute-start | bytes 3145736 | tf_op jit(solution)/shard_map/ppermute | solution.py:18
  47.4 4.7 %fusion.22 = f32[128,3,2048]{0,2,1:T(8,128)S(1)} fusion(f32[130,3,2048]{0,2,1:T(8,128)S(1)} %maximum_convert_fusion, f32[3,2048]{1,0:T(4,128)S(1)} %get-tuple-element.123, f32[3,2048]{1,0:T(4,128)S(1)} %get-tuple-element.124, f32[3,2048]{1,0:T(4,128)S(1)} %get-tuple-element.122), kind=kLoop, calls=%fused_computation.27 | loop fusion | flops 3932160 | bytes 12656640 | tf_op jit(solution)/shard_map/add | solution.py:25
  53.0 2.0 fusion.32
  55.0 2.2 copy.48
  57.2 2.2 collective-permute-done.3
  59.4 5.3 %collective-permute-start.4 = (bf16[128,2,2048]{0,2,1:T(8,128)(2,1)}, bf16[128,2,2048]{0,2,1:T(8,128)(2,1)}, u32[]{:S(2)}, u32[]{:S(2)}) collective-permute-start(bf16[128,2,2048]{0,2,1:T(8,128)(2,1)} %collective-permute-done.3), channel_id=1, source_target_pairs={{0,1},{1,2},{2,3},{3,4},{4,5},{5,6},{6,7},{7,8},{8,9},{9,10},{10,1... | collective-permute-start | bytes 3145736 | tf_op jit(solution)/shard_map/ppermute | solution.py:18
  64.7 16.3 %collective-permute-done.4 = bf16[128,2,2048]{0,2,1:T(8,128)(2,1)} collective-permute-done((bf16[128,2,2048]{0,2,1:T(8,128)(2,1)}, bf16[128,2,2048]{0,2,1:T(8,128)(2,1)}, u32[]{:S(2)}, u32[]{:S(2)}) %collective-permute-start.4) | collective-permute-done | bytes 1048608 | tf_op jit(solution)/shard_map/ppermute | solution.py:18
  80.9 5.3 %collective-permute-start.5 = (bf16[128,2,2048]{0,2,1:T(8,128)(2,1)}, bf16[128,2,2048]{0,2,1:T(8,128)(2,1)}, u32[]{:S(2)}, u32[]{:S(2)}) collective-permute-start(bf16[128,2,2048]{0,2,1:T(8,128)(2,1)} %collective-permute-done.4), channel_id=1, source_target_pairs={{0,1},{1,2},{2,3},{3,4},{4,5},{5,6},{6,7},{7,8},{8,9},{9,10},{10,1... | collective-permute-start | bytes 3145736 | tf_op jit(solution)/shard_map/ppermute | solution.py:18
  87.6 16.3 %collective-permute-done.5 = bf16[128,2,2048]{0,2,1:T(8,128)(2,1)} collective-permute-done((bf16[128,2,2048]{0,2,1:T(8,128)(2,1)}, bf16[128,2,2048]{0,2,1:T(8,128)(2,1)}, u32[]{:S(2)}, u32[]{:S(2)}) %collective-permute-start.5) | collective-permute-done | bytes 1048608 | tf_op jit(solution)/shard_map/ppermute | solution.py:18
  103.9 5.3 %collective-permute-start.6 = (bf16[128,2,2048]{0,2,1:T(8,128)(2,1)}, bf16[128,2,2048]{0,2,1:T(8,128)(2,1)}, u32[]{:S(2)}, u32[]{:S(2)}) collective-permute-start(bf16[128,2,2048]{0,2,1:T(8,128)(2,1)} %collective-permute-done.5), channel_id=1, source_target_pairs={{0,1},{1,2},{2,3},{3,4},{4,5},{5,6},{6,7},{7,8},{8,9},{9,10},{10,1... | collective-permute-start | bytes 3145736 | tf_op jit(solution)/shard_map/ppermute | solution.py:18
  109.9 1.9 slice.52
  111.7 2.0 copy.72
  113.8 1.5 copy.75
  115.5 57.4 %gather_fusion = bf16[16384,128]{1,0:T(8,128)(2,1)} fusion(bf16[128,128]{0,1:T(8,128)(2,1)S(1)} %copy.60, s32[16384]{0:T(1024)S(1)} %fusion.41), kind=kCustom, calls=%fused_computation | custom fusion | bytes 8454144 | tf_op jit(solution)/shard_map/jit(_take)/gather | solution.py:45
  172.9 6.7 %copy.46 = bf16[128,128,128]{1,0,2:T(8,128)(2,1)} copy(bf16[128,128,128]{2,1,0:T(8,128)(2,1)} %bitcast.83) | data formatting | bytes 8388608 | tf_op jit(solution)/shard_map/jit(_take)/gather | solution.py:45
  180.0 2.1 collective-permute-start.7
  182.1 5.7 %fusion.16 = f32[128,16,128]{2,1,0:T(8,128)} fusion(bf16[128,128,16]{0,2,1:T(8,128)(2,1)} %bitcast.88, bf16[128,128,128]{1,0,2:T(8,128)(2,1)} %copy.46, pred[128,128]{1,0:T(8,128)(4,1)S(1)} %get-tuple-element.127, pred[128,128]{1,0:T(8,128)(4,1)S(1)} %get-tuple-element.128), kind=kOutput, calls=%fused_computation.20 | convolution fusion | flops 71303168 | bytes 5799936 | tf_op jit(solution)/shard_map/gts,sgc->tgc/dot_general | solution.py:104
  187.8 2.0 copy.78
  190.3 1.4 copy.68
  191.7 3.0 %convolution_add_fusion = f32[128,16,128]{2,1,0:T(8,128)S(1)} fusion(f32[128,16,128]{2,1,0:T(8,128)} %fusion.16, f32[128,16,16]{1,2,0:T(8,128)} %copy.68, f32[128,16]{1,0:T(8,128)} %copy-done.4, f32[128]{0:T(128)S(1)} %add_convert_fusion, f32[128,16]{1,0:T(8,128)S(1)} %copy.45), kind=kOutput, calls=%fused_computation.35 | convolution fusion | flops 51118080 | bytes 2245120 | tf_op jit(solution)/shard_map/gmt,gmc->tgc/dot_general | solution.py:61
  195.6 2.0 copy.56
  197.7 1.5 constant_dynamic-update-slice_fusion.7
  199.2 1.6 constant_dynamic-update-slice_fusion.6
  200.8 1.6 constant_dynamic-update-slice_fusion.5
  202.4 1.7 constant_dynamic-update-slice_fusion.4
  204.1 1.6 constant_dynamic-update-slice_fusion.3
  205.7 1.6 constant_dynamic-update-slice_fusion.2
  207.3 1.6 constant_dynamic-update-slice_fusion.1
  209.2 3.7 %fusion.50 = (bf16[1024,1,2048]{0,2,1:T(8,128)(2,1)}, bf16[1024,1,2048]{0,2,1:T(8,128)(2,1)}) fusion(bf16[1024,2,2048]{0,2,1:T(8,128)(2,1)S(1)} %constant_dynamic-update-slice_fusion), kind=kLoop, calls=%fused_computation.90 | loop fusion | bytes 16777216 | tf_op jit(solution)/shard_map/slice | solution.py:129
  212.9 45.8 %while.11 = (s32[]{:T(128)}, bf16[16,128,128]{2,1,0:T(8,128)(2,1)S(1)}, bf16[16,128,128]{1,2,0:T(8,128)(2,1)}, bf16[16,1024,128]{1,2,0:T(8,128)(2,1)}, bf16[16,1...) while((s32[]{:T(128)}, ...), condition=%wide.region_6.7_spmd.clone, body=%wide.region_3.6_spmd.clone.sunk | while | flops 68697856 | bytes 2177645 | solution.py:90
  212.9 1.3 fusion.61
  214.5 1.3 fusion.63
  215.8 1.4 fusion.61
  217.4 1.3 fusion.63
  218.7 1.4 fusion.61
  221.5 1.3 fusion.61
  223.1 1.3 fusion.63
  224.4 1.3 fusion.61
  226.0 1.3 fusion.63
  227.3 1.3 fusion.61
  230.1 1.3 fusion.61
  231.7 1.3 fusion.63
  233.0 1.3 fusion.61
  234.6 1.3 fusion.63
  235.9 1.3 fusion.61
  238.7 1.3 fusion.61
  240.3 1.3 fusion.63
  241.6 1.3 fusion.61
  243.2 1.3 fusion.63
  244.5 1.3 fusion.61
  247.3 1.3 fusion.61
  248.9 1.3 fusion.63
  250.2 1.3 fusion.61
  251.8 1.3 fusion.63
  253.1 1.3 fusion.61
  255.9 1.3 fusion.61
  257.5 1.3 fusion.63
  (75 shorter events, 20.0 us)
Async XLA Ops:
  7.2 22.9 %copy-start.6 = (f32[128,16]{0,1:T(8,128)S(1)}, f32[128,16]{0,1:T(8,128)}, u32[]{:S(2)}) copy-start(f32[128,16]{0,1:T(8,128)} %param.10) | copy-start | bytes 24580
  7.2 22.9 %copy-start.7 = (f32[128,16]{0,1:T(8,128)S(1)}, f32[128,16]{0,1:T(8,128)}, u32[]{:S(2)}) copy-start(f32[128,16]{0,1:T(8,128)} %param.11) | copy-start | bytes 24580
  7.2 22.9 %copy-start.5 = (f32[3,3,2048]{2,1,0:T(4,128)S(1)}, f32[3,3,2048]{2,1,0:T(4,128)}, u32[]{:S(2)}) copy-start(f32[3,3,2048]{2,1,0:T(4,128)} %param.9) | copy-start | bytes 221188
  7.2 180.6 %all-gather.3.cloned.1.call-start = ((), (), s32[]{:S(2)}) async-start(), calls=%async_computation | async-start | bytes 2228224 | tf_op jit(solution)/shard_map/all_gather | solution.py:108
  9.2 20.9 %copy-start = (bf16[128,2,2048]{0,2,1:T(8,128)(2,1)}, bf16[128,2,2048]{0,2,1:T(8,128)(2,1)S(1)}, u32[]{:S(2)}) copy-start(bf16[128,2,2048]{0,2,1:T(8,128)(2,1)S(1)} %copy.73) | copy-start | bytes 3145732
  9.2 15.4 %collective-permute-start.1 = (bf16[128,2,2048]{0,2,1:T(8,128)(2,1)S(1)}, bf16[128,2,2048]{0,2,1:T(8,128)(2,1)}, u32[]{:S(2)}, u32[]{:S(2)}) collective-permute-start(bf16[128,2,2048]{0,2,1:T(8,128)(2,1)S(1)} %copy.73), channel_id=1, source_target_pairs={{0,1},{1,2},{2,3},{3,4},{4,5},{5,6},{6,7},{7,8},{8,9},{9,10},{10,1... | collective-permute-start | bytes 3145736 | tf_op jit(solution)/shard_map/ppermute | solution.py:18
  13.9 18.3 %collective-permute-start = (bf16[2,3,2048]{2,0,1:T(2,128)(2,1)S(1)}, bf16[2,3,2048]{2,0,1:T(2,128)(2,1)S(1)}, u32[]{:S(2)}, u32[]{:S(2)}) collective-permute-start(bf16[2,3,2048]{2,0,1:T(2,128)(2,1)S(1)} %slice.43), channel_id=1, source_target_pairs={{0,1},{1,2},{2,3},{3,4},{4,5},{5,6},{6,7},{7,8},{8,9},{9,10},{10,1... | collective-permute-start | bytes 73736 | tf_op jit(solution)/shard_map/ppermute | solution.py:18
  24.7 17.4 %collective-permute-start.2 = (bf16[128,2,2048]{0,2,1:T(8,128)(2,1)}, bf16[128,2,2048]{0,2,1:T(8,128)(2,1)}, u32[]{:S(2)}, u32[]{:S(2)}) collective-permute-start(bf16[128,2,2048]{0,2,1:T(8,128)(2,1)} %collective-permute-done.1), channel_id=1, source_target_pairs={{0,1},{1,2},{2,3},{3,4},{4,5},{5,6},{6,7},{7,8},{8,9},{9,10},{10,1... | collective-permute-start | bytes 3145736 | tf_op jit(solution)/shard_map/ppermute | solution.py:18
  42.1 17.3 %collective-permute-start.3 = (bf16[128,2,2048]{0,2,1:T(8,128)(2,1)}, bf16[128,2,2048]{0,2,1:T(8,128)(2,1)}, u32[]{:S(2)}, u32[]{:S(2)}) collective-permute-start(bf16[128,2,2048]{0,2,1:T(8,128)(2,1)} %collective-permute-done.2), channel_id=1, source_target_pairs={{0,1},{1,2},{2,3},{3,4},{4,5},{5,6},{6,7},{7,8},{8,9},{9,10},{10,1... | collective-permute-start | bytes 3145736 | tf_op jit(solution)/shard_map/ppermute | solution.py:18
  52.2 0.8 copy-start.2
  59.4 21.5 %collective-permute-start.4 = (bf16[128,2,2048]{0,2,1:T(8,128)(2,1)}, bf16[128,2,2048]{0,2,1:T(8,128)(2,1)}, u32[]{:S(2)}, u32[]{:S(2)}) collective-permute-start(bf16[128,2,2048]{0,2,1:T(8,128)(2,1)} %collective-permute-done.3), channel_id=1, source_target_pairs={{0,1},{1,2},{2,3},{3,4},{4,5},{5,6},{6,7},{7,8},{8,9},{9,10},{10,1... | collective-permute-start | bytes 3145736 | tf_op jit(solution)/shard_map/ppermute | solution.py:18
  80.9 23.0 %collective-permute-start.5 = (bf16[128,2,2048]{0,2,1:T(8,128)(2,1)}, bf16[128,2,2048]{0,2,1:T(8,128)(2,1)}, u32[]{:S(2)}, u32[]{:S(2)}) collective-permute-start(bf16[128,2,2048]{0,2,1:T(8,128)(2,1)} %collective-permute-done.4), channel_id=1, source_target_pairs={{0,1},{1,2},{2,3},{3,4},{4,5},{5,6},{6,7},{7,8},{8,9},{9,10},{10,1... | collective-permute-start | bytes 3145736 | tf_op jit(solution)/shard_map/ppermute | solution.py:18
  86.3 25.4 %copy-start.4 = (f32[128,16]{1,0:T(8,128)}, f32[128,16]{1,0:T(8,128)S(1)}, u32[]{:S(2)}) copy-start(f32[128,16]{1,0:T(8,128)S(1)} %copy.74) | copy-start | bytes 24580
  103.9 76.0 %collective-permute-start.6 = (bf16[128,2,2048]{0,2,1:T(8,128)(2,1)}, bf16[128,2,2048]{0,2,1:T(8,128)(2,1)}, u32[]{:S(2)}, u32[]{:S(2)}) collective-permute-start(bf16[128,2,2048]{0,2,1:T(8,128)(2,1)} %collective-permute-done.5), channel_id=1, source_target_pairs={{0,1},{1,2},{2,3},{3,4},{4,5},{5,6},{6,7},{7,8},{8,9},{9,10},{10,1... | collective-permute-start | bytes 3145736 | tf_op jit(solution)/shard_map/ppermute | solution.py:18
  172.9 6.7 %copy-start.8 = (s32[4]{0:T(128)S(1)}, s32[4]{0:T(128)}, u32[]{:S(2)}) copy-start(s32[4]{0:T(128)} %param.13) | copy-start | bytes 52
  180.0 17.7 %collective-permute-start.7 = (bf16[128,2,2048]{0,2,1:T(8,128)(2,1)}, bf16[128,2,2048]{0,2,1:T(8,128)(2,1)}, u32[]{:S(2)}, u32[]{:S(2)}) collective-permute-start(bf16[128,2,2048]{0,2,1:T(8,128)(2,1)} %collective-permute-done.6), channel_id=1, source_target_pairs={{0,1},{1,2},{2,3},{3,4},{4,5},{5,6},{6,7},{7,8},{8,9},{9,10},{10,1... | collective-permute-start | bytes 3145736 | tf_op jit(solution)/shard_map/ppermute | solution.py:18
  202.4 6.5 %copy-start.1 = (bf16[128,2,2048]{0,2,1:T(8,128)(2,1)S(1)}, bf16[128,2,2048]{0,2,1:T(8,128)(2,1)}, u32[]{:S(2)}) copy-start(bf16[128,2,2048]{0,2,1:T(8,128)(2,1)} %copy-done) | copy-start | bytes 3145732
  209.2 3.7 %copy-start.3 = (bf16[16,128,128]{2,1,0:T(8,128)(2,1)S(1)}, bf16[16,128,128]{2,1,0:T(8,128)(2,1)}, u32[]{:S(2)}) copy-start(bf16[16,128,128]{2,1,0:T(8,128)(2,1)} %custom-call.3) | copy-start | bytes 1572868
Sparse Core Ops, SparseCore 0:
  57.4 44.4 all-gather.2
where the time goes:
time: 268 us; the launch traced here: 267 us
  local copies, waits for them, and re-layouts  100 us (37%)
  matrix products  52.4 us (20%)
  waiting for transfers between devices  51.5 us (19%)
  starting transfers between devices  34.3 us (13%)
  between operations  14.4 us (5%)
  other arithmetic  13.5 us (5%)
    gather x2, local copies, waits for them, and re-layouts, toeplitz(): jnp.take(filter_taps, jnp.clip(lag_index, 0, row_count - 1), axis=1)  64 us
    ppermute x8, waiting for transfers between devices, from_behind(): lax.ppermute(value, axis, [(source, source + steps) for source in range(i...  51.5 us
    ppermute x8, starting transfers between devices, from_behind(): lax.ppermute(value, axis, [(source, source + steps) for source in range(i...  34.2 us
    unnamed x32, local copies, waits for them, and re-layouts  22.2 us
    dot_general x16, matrix products, one_head(): jnp.dot(query_rows, key_rows.T, preferred_element_type=jnp.float32)  21.6 us
    dot_general x16, matrix products, one_head(): jnp.dot(weight, value_rows, preferred_element_type=jnp.float32)  20.2 us
    dot_general x1, matrix products, on_device(): jnp.einsum('gts,sgc->tgc', toeplitz(filter_taps), grouped, preferred_elem...  5.66 us
    slice x2, local copies, waits for them, and re-layouts, on_device(): attn_out = attend(attn_qkv[:, 0], window[:, 0], window[:, 1], allowed)  5.59 us
  transfers between devices with their start and end apart: 9, of which 5 were waited for; matrix products, arithmetic and copies ran while one was open for 38% of the time, Pallas kernels for 0%

commit v1 on v0

--- a/solution.py
+++ b/solution.py
@@ -1,8 +1,11 @@
+import functools
 import math
 
 import jax
 import jax.numpy as jnp
 from jax import lax
+from jax.experimental import pallas as pl
+from jax.experimental.pallas import tpu as pltpu
 from jax.sharding import PartitionSpec as P
 
 HEAD = 128
@@ -62,7 +65,9 @@
 
 
 def visible(query_pos, key_pos, doc_lengths):
-    bounds = jnp.cumsum(doc_lengths, dtype=jnp.int32)
+    docs = doc_lengths.shape[0]
+    upto = jnp.arange(docs)[:, None] >= jnp.arange(docs)[None, :]
+    bounds = jnp.sum(jnp.where(upto, doc_lengths[None, :], 0), axis=1)
     query_doc = jnp.sum((query_pos[:, None] >= bounds[None, :]).astype(jnp.int32), axis=1)
     key_doc = jnp.sum((key_pos[:, None] >= bounds[None, :]).astype(jnp.int32), axis=1)
     causal = (key_pos[None, :] <= query_pos[:, None]) & (key_pos[None, :] >= 0)
@@ -130,6 +135,437 @@
     return (hyena_out, attn_out)
 
 
+LANES = 128
+PLANE = 4
+EDGE = 16
+
+
+def fused_kernel(
+    n,
+    hq,
+    short_weight,
+    rate_t,
+    residue_t,
+    docs,
+    aq,
+    hyena_out,
+    attn_out,
+    gath,
+    obuf,
+    prev,
+    query,
+    near,
+    far_powers,
+    rate_c,
+    own_state,
+    state_send,
+    state_in,
+    total_send,
+    total_in,
+    sem_q_send,
+    sem_q_recv,
+    sem_o_send,
+    sem_o_recv,
+    sem_edge,
+    sem_s_send,
+    sem_s_recv,
+    sem_t_send,
+    sem_t_recv,
+):
+    rows = hq.shape[1]
+    modes = rate_t.shape[0]
+    groups = rate_t.shape[1]
+    channels = hq.shape[2]
+    width = channels // groups
+    per_tile = LANES // width
+    tiles = channels // LANES
+    planes = n // PLANE
+    me = lax.axis_index("ctx")
+    plane = me // PLANE
+    spot = lax.rem(me, PLANE)
+
+    def remote(src, dst, send_sem, recv_sem, target):
+        return pltpu.make_async_remote_copy(
+            src_ref=src,
+            dst_ref=dst,
+            send_sem=send_sem,
+            recv_sem=recv_sem,
+            device_id={"ctx": target},
+            device_id_type=pl.DeviceIdType.MESH,
+        )
+
+    def head_columns(h):
+        return pl.ds(pl.multiple_of(h * HEAD, HEAD), HEAD)
+
+    def send_head(h, slot):
+        return remote(
+            aq.at[:, :, head_columns(h)],
+            gath.at[slot],
+            sem_q_send.at[h],
+            sem_q_recv.at[slot],
+            h,
+        )
+
+    def send_out(b, slot):
+        return remote(
+            obuf.at[b],
+            attn_out.at[:, head_columns(slot)],
+            sem_o_send.at[b],
+            sem_o_recv.at[slot],
+            b,
+        )
+
+    def send_edge():
+        return remote(
+            hq.at[:, pl.ds(rows - EDGE, EDGE), :],
+            prev,
+            sem_edge.at[0],
+            sem_edge.at[1],
+            lax.rem(me + 1, n),
+        )
+
+    def send_state(target_spot, slot):
+        return remote(
+            state_send,
+            state_in.at[slot],
+            sem_s_send.at[target_spot],
+            sem_s_recv.at[slot],
+            plane * PLANE + target_spot,
+        )
+
+    def send_total(target_plane, slot):
+        return remote(
+            total_send,
+            total_in.at[slot],
+            sem_t_send.at[target_plane],
+            sem_t_recv.at[slot],
+            target_plane * PLANE + spot,
+        )
+
+    barrier = pltpu.get_barrier_semaphore()
+
+    @pl.loop(1, n)
+    def _(k):
+        pl.semaphore_signal(
+            barrier,
+            inc=1,
+            device_id={"ctx": lax.rem(me + k, n)},
+            device_id_type=pl.DeviceIdType.MESH,
+        )
+
+    pl.semaphore_wait(barrier, n - 1)
+
+    @pl.when(me < n - 1)
+    def _():
+        send_edge().start()
+
+    @pl.loop(1, n)
+    def _(k):
+        send_head(lax.rem(me + k, n), me).start()
+
+    own_heads = pltpu.make_async_copy(
+        aq.at[:, :, head_columns(me)], gath.at[me], sem_q_recv.at[me]
+    )
+    own_heads.start()
+
+    @pl.when(me == 0)
+    def _():
+        prev[...] = jnp.zeros_like(prev)
+
+    @pl.when(me > 0)
+    def _():
+        send_edge().wait_recv()
+
+    lane = lax.broadcasted_iota(jnp.int32, (1, LANES), 1)
+    sub = lax.broadcasted_iota(jnp.int32, (LANES, 1), 0)
+    own_block = (sub // width) == (lane // width)
+    row_col = lax.broadcasted_iota(jnp.int32, (rows, 1), 0)
+    row_f = row_col.astype(jnp.float32)
+    key_row = lax.broadcasted_iota(jnp.int32, (1, rows), 1)
+    lower = key_row <= row_col
+    mode_pick = lax.broadcasted_iota(jnp.int32, (modes, 1), 0) == lax.rem(lane, modes)
+    rev_f = lax.rem(rows - row_col, rows).astype(jnp.float32)
+    filter_of = (
+        lax.broadcasted_iota(jnp.int32, (per_tile, 1), 0) == lane // width
+    ).astype(jnp.float32)
+
+    @pl.loop(0, tiles)
+    def _(i):
+        at = pl.ds(pl.multiple_of(i * LANES, LANES), LANES)
+
+        def feature(j):
+            value = jnp.concatenate([prev[j, :, at], hq[j, :, at]], axis=0).astype(jnp.float32)
+            one = pltpu.roll(value, 1, 0)
+            two = pltpu.roll(value, 2, 0)
+            return (
+                short_weight[0, pl.ds(j, 1), at] * value[EDGE:]
+                + short_weight[1, pl.ds(j, 1), at] * one[EDGE:]
+                + short_weight[2, pl.ds(j, 1), at] * two[EDGE:]
+            )
+
+        query[:, at] = feature(0)
+        mixed_f = feature(1) * feature(2)
+        mixed_b = mixed_f.astype(jnp.bfloat16)
+        mixed_in = mixed_b.astype(jnp.float32)
+
+        pick = (
+            lax.broadcasted_iota(jnp.int32, (groups, LANES), 0)
+            == i * per_tile + lane // width
+        ).astype(jnp.float32)
+        rates = jnp.dot(rate_t[...], pick, precision=precise, preferred_element_type=jnp.float32)
+        residues = jnp.dot(
+            residue_t[...], pick, precision=precise, preferred_element_type=jnp.float32
+        )
+        coeffs = residues * jnp.sqrt(2.0 * rates / modes)
+        rate_c[:, at] = rates
+        rate_row = jnp.sum(jnp.where(mode_pick, rates, 0.0), axis=0, keepdims=True)
+        coeff_row = jnp.sum(jnp.where(mode_pick, coeffs, 0.0), axis=0, keepdims=True)
+
+        ends = jnp.exp(-rate_row * (rows - 1 - row_f))
+        full = lax.dot_general(
+            ends,
+            mixed_in,
+            (((0,), (0,)), ((), ())),
+            precision=precise,
+            preferred_element_type=jnp.float32,
+        )
+        full = jnp.where(own_block, full, 0.0).reshape(per_tile, modes, LANES)
+        state = jnp.sum(full, axis=0)
+        own_state[:, at] = state
+        state_send[:, at] = state.astype(jnp.bfloat16)
+        far_powers[:, at] = coeff_row * jnp.exp(-rate_row * (row_f + 1.0))
+
+        taps_powers = coeff_row * jnp.exp(-rate_row * rev_f)
+        taps = lax.dot_general(
+            filter_of,
+            taps_powers,
+            (((1,), (1,)), ((), ())),
+            precision=precise,
+            preferred_element_type=jnp.float32,
+        )
+        tables = []
+        inputs = []
+        for g in range(per_tile):
+            spread = jnp.broadcast_to(taps[g : g + 1, :], (rows, rows))
+            table = pltpu.roll(spread, 0, 1, stride=1, stride_axis=0)
+            tables.append(jnp.where(lower, table, 0.0).astype(jnp.bfloat16))
+            inputs.append(jnp.where(lane // width == g, mixed_in, 0.0).astype(jnp.bfloat16))
+        near[:, at] = jnp.dot(
+            jnp.concatenate(tables, axis=1),
+            jnp.concatenate(inputs, axis=0),
+            preferred_element_type=jnp.float32,
+        )
+
+    for other in range(PLANE):
+
+        @pl.when(spot != other)
+        def _(other=other):
+            send_state(other, spot).start()
+
+    def decay(steps):
+        return jnp.exp(rate_c[...] * (-float(rows) * steps.astype(jnp.float32)))
+
+    own_state[...] = decay(PLANE - 1 - spot) * own_state[...]
+    for other in range(PLANE):
+
+        @pl.when(spot != other)
+        def _(other=other):
+            send_state(other, other).wait_recv()
+            own_state[...] += decay(jnp.int32(PLANE - 1 - other)) * state_in[other].astype(
+                jnp.float32
+            )
+
+    total_send[...] = own_state[...].astype(jnp.bfloat16)
+    for later in range(planes):
+
+        @pl.when(plane < later)
+        def _(later=later):
+            send_total(later, plane).start()
+
+    bounds = []
+    running = jnp.int32(0)
+    for k in range(docs.shape[0]):
+        running = running + docs[k]
+        bounds.append(running)
+    scale = 1.0 / math.sqrt(HEAD)
+    span = min(SPAN, n)
+    head_row = lax.broadcasted_iota(jnp.int32, (rows, 1), 0)
+    window_row = lax.broadcasted_iota(jnp.int32, (1, span * rows), 1)
+
+    def wait_head(b):
+        @pl.when(b != me)
+        def _():
+            send_head(b, b).wait_recv()
+
+        @pl.when(b == me)
+        def _():
+            own_heads.wait()
+
+    def attend_block(b):
+        begin = jnp.maximum(b - (span - 1), 0)
+        keys = gath[pl.ds(begin, span), 1].reshape(span * rows, HEAD)
+        values = gath[pl.ds(begin, span), 2].reshape(span * rows, HEAD)
+        scores = lax.dot_general(
+            gath[b, 0], keys, (((1,), (1,)), ((), ())), preferred_element_type=jnp.float32
+        )
+        query_pos = b * rows + head_row
+        first = jnp.zeros_like(query_pos)
+        for bound in bounds:
+            first = jnp.where(query_pos >= bound, bound, first)
+        key_pos = begin * rows + window_row
+        allowed = (key_pos <= query_pos) & (key_pos >= first)
+        scores = jnp.where(allowed, scores, -jnp.inf)
+        row_max = jnp.max(scores, axis=1, keepdims=True)
+        exp_scores = jnp.exp((scores - row_max) * scale)
+        row_sum = jnp.sum(exp_scores, axis=1, keepdims=True)
+        mixed_values = jnp.dot(
+            exp_scores.astype(jnp.bfloat16), values, preferred_element_type=jnp.float32
+        )
+        obuf[b] = (mixed_values / row_sum).astype(jnp.bfloat16)
+
+        @pl.when(b != me)
+        def _():
+            send_out(b, me).start()
+
+        @pl.when(b == me)
+        def _():
+            pltpu.make_async_copy(
+                obuf.at[b], attn_out.at[:, head_columns(me)], sem_o_recv.at[me]
+            ).start()
+
+    @pl.loop(0, span)
+    def _(b):
+        wait_head(b)
+
+    @pl.loop(0, span)
+    def _(b):
+        attend_block(b)
+
+    @pl.loop(span, n)
+    def _(b):
+        wait_head(b)
+        attend_block(b)
+
+    own_state[...] = jnp.zeros(own_state.shape, jnp.float32)
+    for earlier in range(planes):
+
+        @pl.when(earlier < plane)
+        def _(earlier=earlier):
+            send_total(earlier, earlier).wait_recv()
+            steps = PLANE * (plane - 1 - earlier) + spot
+            own_state[...] += decay(steps) * total_in[earlier].astype(jnp.float32)
+
+    for other in range(PLANE):
+
+        @pl.when(other < spot)
+        def _(other=other):
+            own_state[...] += decay(spot - 1 - other) * state_in[other].astype(jnp.float32)
+
+    @pl.loop(0, tiles)
+    def _(i):
+        at = pl.ds(pl.multiple_of(i * LANES, LANES), LANES)
+        carried = jnp.concatenate([own_state[:, at]] * per_tile, axis=0)
+        carried = jnp.where(own_block, carried, 0.0)
+        far = jnp.dot(
+            far_powers[:, at], carried, precision=precise, preferred_element_type=jnp.float32
+        )
+        hyena_out[:, at] = (query[:, at] * (near[:, at] + far)).astype(jnp.bfloat16)
+
+    @pl.when(me < n - 1)
+    def _():
+        send_edge().wait_send()
+
+    for other in range(PLANE):
+
+        @pl.when(spot != other)
+        def _(other=other):
+            send_state(other, spot).wait_send()
+
+    for later in range(planes):
+
+        @pl.when(plane < later)
+        def _(later=later):
+            send_total(later, plane).wait_send()
+
+    @pl.loop(0, n)
+    def _(b):
+        @pl.when(b != me)
+        def _():
+            send_head(b, me).wait_send()
+            send_out(b, me).wait_send()
+            send_out(b, b).wait_recv()
+
+        @pl.when(b == me)
+        def _():
+            pltpu.make_async_copy(
+                obuf.at[b], attn_out.at[:, head_columns(me)], sem_o_recv.at[me]
+            ).wait()
+
+
+def by_heads(n, hyena_qkv, short_weight, filter_rate, filter_residue, attn_qkv, doc_lengths):
+    rows, streams, channels = hyena_qkv.shape
+    modes = filter_rate.shape[1]
+    out = jax.ShapeDtypeStruct((rows, channels), jnp.bfloat16)
+    vmem = pl.BlockSpec(memory_space=pltpu.VMEM)
+    dma = pltpu.SemaphoreType.DMA
+    bf16, f32 = jnp.bfloat16, jnp.float32
+    return pl.pallas_call(
+        functools.partial(fused_kernel, n),
+        out_shape=(out, out),
+        in_specs=[vmem] * 4
+        + [pl.BlockSpec(memory_space=pltpu.SMEM), pl.BlockSpec(memory_space=pl.ANY)],
+        out_specs=(vmem, vmem),
+        scratch_shapes=[
+            pltpu.VMEM((n, streams, rows, HEAD), bf16),
+            pltpu.VMEM((n, rows, HEAD), bf16),
+            pltpu.VMEM((streams, EDGE, channels), bf16),
+            pltpu.VMEM((rows, channels), f32),
+            pltpu.VMEM((rows, channels), f32),
+            pltpu.VMEM((rows, channels), f32),
+            pltpu.VMEM((modes, channels), f32),
+            pltpu.VMEM((modes, channels), f32),
+            pltpu.VMEM((modes, channels), bf16),
+            pltpu.VMEM((PLANE, modes, channels), bf16),
+            pltpu.VMEM((modes, channels), bf16),
+            pltpu.VMEM((n // PLANE, modes, channels), bf16),
+            dma((n,)),
+            dma((n,)),
+            dma((n,)),
+            dma((n,)),
+            dma((2,)),
+            dma((PLANE,)),
+            dma((PLANE,)),
+            dma((n // PLANE,)),
+            dma((n // PLANE,)),
+        ],
+        compiler_params=pltpu.CompilerParams(
+            collective_id=0, has_side_effects=True, vmem_limit_bytes=48 * 2**20
+        ),
+    )(
+        hyena_qkv.transpose(1, 0, 2),
+        short_weight,
+        filter_rate.T,
+        filter_residue.T,
+        doc_lengths,
+        attn_qkv.transpose(1, 0, 2),
+    )
+
+
+def on_any_slice(hyena_qkv, short_weight, filter_rate, filter_residue, attn_qkv, doc_lengths):
+    n = lax.axis_size("ctx")
+    rows, _, channels = hyena_qkv.shape
+    groups, modes = filter_rate.shape
+    fits = (
+        channels == n * HEAD
+        and n % PLANE == 0
+        and channels == groups * modes
+        and LANES % modes == 0
+        and rows == LANES
+    )
+    args = (hyena_qkv, short_weight, filter_rate, filter_residue, attn_qkv, doc_lengths)
+    return by_heads(n, *args) if fits else on_device(*args)
+
+
 def solution(mesh):
     in_specs = (
         P(("group", "ctx"), None, None),
@@ -141,5 +577,5 @@
     )
     out_specs = (P(("group", "ctx"), None), P(("group", "ctx"), None))
     return jax.shard_map(
-        on_device, mesh=mesh, in_specs=in_specs, out_specs=out_specs, check_vma=False
-    )
+        on_any_slice, mesh=mesh, in_specs=in_specs, out_specs=out_specs, check_vma=False
+    )

time: 268 us -> 72.3 us (0.27)
  the two profiles are of different devices: /device:TPU:13 before, /device:TPU:29 now
where the time goes in v1:
time: 72.3 us; the launch traced here: 72 us
  Pallas kernels  64 us (89%)
  local copies, waits for them, and re-layouts  7.34 us (10%)
    pallas_call x1, Pallas kernels, by_heads(): pl.pallas_call(functools.partial(fused_kernel, n), out_shape=(out, out),...  64 us
    unnamed x14, local copies, waits for them, and re-layouts  7.34 us

profile of v1, /device:TPU:29, one launch (start us, length us, event | category | flops | bytes accessed | tf_op | source)
XLA Modules:
  0.0 72.0 jit_solution(13761085245197664716)
XLA Ops:
  0.6 0.0 copy-start
  0.6 1.4 %copy-done = bf16[128,3,2048]{2,0,1:T(8,128)(2,1)S(1)} copy-done((bf16[128,3,2048]{2,0,1:T(8,128)(2,1)S(1)}, bf16[128,3,2048]{2,0,1:T(8,128)(2,1)}, u32[]{:S(2)}) %copy-start) | copy-done | bytes 1572888
  2.0 0.0 copy-start.1
  2.0 1.4 %copy-done.1 = bf16[128,3,2048]{2,0,1:T(8,128)(2,1)S(1)} copy-done((bf16[128,3,2048]{2,0,1:T(8,128)(2,1)S(1)}, bf16[128,3,2048]{2,0,1:T(8,128)(2,1)}, u32[]{:S(2)}) %copy-start.1) | copy-done | bytes 1572888
  3.4 0.0 copy-start.2
  3.5 0.9 %copy-done.2 = f32[3,3,2048]{2,1,0:T(4,128)S(1)} copy-done((f32[3,3,2048]{2,1,0:T(4,128)S(1)}, f32[3,3,2048]{2,1,0:T(4,128)}, u32[]{:S(2)}) %copy-start.2) | copy-done | bytes 73752
  4.3 0.0 copy-start.3
  4.3 0.7 copy-done.3
  5.0 0.0 copy-start.4
  5.0 0.7 copy-done.4
  5.7 0.0 copy-start.5
  5.7 0.7 copy-done.5
  6.4 64.0 %shard_map.77 = (bf16[128,2048]{1,0:T(8,128)(2,1)S(1)}, bf16[128,2048]{1,0:T(8,128)(2,1)S(1)}) custom-call(bf16[3,128,2048]{2,1,0:T(8,128)(2,1)S(1)} %bitcast.4, f32[3,3,2048]{2,1,0:T(4,128)S(1)} %copy-done.2, f32[16,128]{1,0:T(8,128)S(1)} %bitcast.6, f32[16,128]{1,0:T(8,128)S(1)} %bitcast.7, s32[4]{0:T(128)S(1)} %copy-done.5, bf16[3,128,2048]{2,1,0:T(8,128)(2,1)S(1)} %bitcast.5), custom_call_target="tpu_custom_call" | custom-call | tf_op jit(solution)/shard_map/pallas_call | solution.py:512
  70.4 0.8 %copy.10 = bf16[128,2048]{1,0:T(8,128)(2,1)} copy(bf16[128,2048]{1,0:T(8,128)(2,1)S(1)} %get-tuple-element.4) | data formatting | bytes 1048576
  71.2 0.8 %copy.11 = bf16[128,2048]{1,0:T(8,128)(2,1)} copy(bf16[128,2048]{1,0:T(8,128)(2,1)S(1)} %get-tuple-element.5) | data formatting | bytes 1048576
Async XLA Ops:
  0.6 1.4 %copy-start = (bf16[128,3,2048]{2,0,1:T(8,128)(2,1)S(1)}, bf16[128,3,2048]{2,0,1:T(8,128)(2,1)}, u32[]{:S(2)}) copy-start(bf16[128,3,2048]{2,0,1:T(8,128)(2,1)} %param.6) | copy-start | bytes 4718596
  2.0 1.4 %copy-start.1 = (bf16[128,3,2048]{2,0,1:T(8,128)(2,1)S(1)}, bf16[128,3,2048]{2,0,1:T(8,128)(2,1)}, u32[]{:S(2)}) copy-start(bf16[128,3,2048]{2,0,1:T(8,128)(2,1)} %param.10) | copy-start | bytes 4718596
  3.4 0.9 %copy-start.2 = (f32[3,3,2048]{2,1,0:T(4,128)S(1)}, f32[3,3,2048]{2,1,0:T(4,128)}, u32[]{:S(2)}) copy-start(f32[3,3,2048]{2,1,0:T(4,128)} %short_weight.1) | copy-start | bytes 221188
  4.3 0.7 copy-start.3
  5.0 0.7 copy-start.4
  5.7 0.7 copy-start.5

commit v2 on v1

--- a/solution.py
+++ b/solution.py
@@ -142,18 +142,25 @@
 
 def fused_kernel(
     n,
+    hq_hbm,
+    short_hbm,
+    rate_hbm,
+    residue_hbm,
+    docs_hbm,
+    aq,
+    hyena_out,
+    attn_out,
     hq,
     short_weight,
     rate_t,
     residue_t,
     docs,
-    aq,
-    hyena_out,
-    attn_out,
     gath,
     obuf,
     prev,
-    query,
+    mixed,
+    rate_rows,
+    coeff_rows,
     near,
     far_powers,
     rate_c,
@@ -171,6 +178,7 @@
     sem_s_recv,
     sem_t_send,
     sem_t_recv,
+    sem_in,
 ):
     rows = hq.shape[1]
     modes = rate_t.shape[0]
@@ -200,7 +208,7 @@
     def send_head(h, slot):
         return remote(
             aq.at[:, :, head_columns(h)],
-            gath.at[slot],
+            gath.at[slot + pad],
             sem_q_send.at[h],
             sem_q_recv.at[slot],
             h,
@@ -217,7 +225,7 @@
 
     def send_edge():
         return remote(
-            hq.at[:, pl.ds(rows - EDGE, EDGE), :],
+            hq_hbm.at[:, pl.ds(rows - EDGE, EDGE), :],
             prev,
             sem_edge.at[0],
             sem_edge.at[1],
@@ -242,6 +250,21 @@
             target_plane * PLANE + spot,
         )
 
+    loads = [
+        pltpu.make_async_copy(source, target, sem_in.at[k])
+        for k, (source, target) in enumerate(
+            (
+                (hq_hbm, hq),
+                (short_hbm, short_weight),
+                (rate_hbm, rate_t),
+                (residue_hbm, residue_t),
+                (docs_hbm, docs),
+            )
+        )
+    ]
+    for load in loads:
+        load.start()
+
     barrier = pltpu.get_barrier_semaphore()
 
     @pl.loop(1, n)
@@ -259,14 +282,20 @@
     def _():
         send_edge().start()
 
-    @pl.loop(1, n)
+    early = n // 2
+    pad = min(SPAN, n) - 1
+
+    @pl.loop(1, early)
     def _(k):
-        send_head(lax.rem(me + k, n), me).start()
+        send_head(lax.rem(me + n - k, n), me).start()
 
     own_heads = pltpu.make_async_copy(
-        aq.at[:, :, head_columns(me)], gath.at[me], sem_q_recv.at[me]
+        aq.at[:, :, head_columns(me)], gath.at[me + pad], sem_q_recv.at[me]
     )
     own_heads.start()
+
+    for p in range(pad):
+        gath[p] = jnp.zeros(gath.shape[1:], gath.dtype)
 
     @pl.when(me == 0)
     def _():
@@ -275,6 +304,9 @@
     @pl.when(me > 0)
     def _():
         send_edge().wait_recv()
+
+    for load in loads:
+        load.wait()
 
     lane = lax.broadcasted_iota(jnp.int32, (1, LANES), 1)
     sub = lax.broadcasted_iota(jnp.int32, (LANES, 1), 0)
@@ -289,21 +321,23 @@
         lax.broadcasted_iota(jnp.int32, (per_tile, 1), 0) == lane // width
     ).astype(jnp.float32)
 
+    def feature_at(j, at):
+        value = jnp.concatenate([prev[j, :, at], hq[j, :, at]], axis=0).astype(jnp.float32)
+        one = pltpu.roll(value, 1, 0)
+        two = pltpu.roll(value, 2, 0)
+        return (
+            short_weight[0, pl.ds(j, 1), at] * value[EDGE:]
+            + short_weight[1, pl.ds(j, 1), at] * one[EDGE:]
+            + short_weight[2, pl.ds(j, 1), at] * two[EDGE:]
+        )
+
     @pl.loop(0, tiles)
     def _(i):
         at = pl.ds(pl.multiple_of(i * LANES, LANES), LANES)
 
         def feature(j):
-            value = jnp.concatenate([prev[j, :, at], hq[j, :, at]], axis=0).astype(jnp.float32)
-            one = pltpu.roll(value, 1, 0)
-            two = pltpu.roll(value, 2, 0)
-            return (
-                short_weight[0, pl.ds(j, 1), at] * value[EDGE:]
-                + short_weight[1, pl.ds(j, 1), at] * one[EDGE:]
-                + short_weight[2, pl.ds(j, 1), at] * two[EDGE:]
-            )
-
-        query[:, at] = feature(0)
+            return feature_at(j, at)
+
         mixed_f = feature(1) * feature(2)
         mixed_b = mixed_f.astype(jnp.bfloat16)
         mixed_in = mixed_b.astype(jnp.float32)
@@ -335,6 +369,25 @@
         state_send[:, at] = state.astype(jnp.bfloat16)
         far_powers[:, at] = coeff_row * jnp.exp(-rate_row * (row_f + 1.0))
 
+        mixed[:, at] = mixed_b
+        rate_rows[:, at] = jnp.broadcast_to(rate_row, (8, LANES))
+        coeff_rows[:, at] = jnp.broadcast_to(coeff_row, (8, LANES))
+
+    for other in range(PLANE):
+
+        @pl.when(spot != other)
+        def _(other=other):
+            send_state(other, spot).start()
+
+    @pl.loop(early, n)
+    def _(k):
+        send_head(lax.rem(me + n - k, n), me).start()
+
+    def near_tile(i):
+        at = pl.ds(pl.multiple_of(i * LANES, LANES), LANES)
+        mixed_in = mixed[:, at].astype(jnp.float32)
+        rate_row = rate_rows[pl.ds(0, 1), at]
+        coeff_row = coeff_rows[pl.ds(0, 1), at]
         taps_powers = coeff_row * jnp.exp(-rate_row * rev_f)
         taps = lax.dot_general(
             filter_of,
@@ -356,11 +409,11 @@
             preferred_element_type=jnp.float32,
         )
 
-    for other in range(PLANE):
-
-        @pl.when(spot != other)
-        def _(other=other):
-            send_state(other, spot).start()
+    first_tiles = (tiles * 16) // 16
+
+    @pl.loop(0, first_tiles)
+    def _(i):
+        near_tile(i)
 
     def decay(steps):
         return jnp.exp(rate_c[...] * (-float(rows) * steps.astype(jnp.float32)))
@@ -392,21 +445,12 @@
     head_row = lax.broadcasted_iota(jnp.int32, (rows, 1), 0)
     window_row = lax.broadcasted_iota(jnp.int32, (1, span * rows), 1)
 
-    def wait_head(b):
-        @pl.when(b != me)
-        def _():
-            send_head(b, b).wait_recv()
-
-        @pl.when(b == me)
-        def _():
-            own_heads.wait()
-
     def attend_block(b):
-        begin = jnp.maximum(b - (span - 1), 0)
-        keys = gath[pl.ds(begin, span), 1].reshape(span * rows, HEAD)
-        values = gath[pl.ds(begin, span), 2].reshape(span * rows, HEAD)
+        begin = b - pad
+        keys = gath[pl.ds(b, span), 1].reshape(span * rows, HEAD)
+        values = gath[pl.ds(b, span), 2].reshape(span * rows, HEAD)
         scores = lax.dot_general(
-            gath[b, 0], keys, (((1,), (1,)), ((), ())), preferred_element_type=jnp.float32
+            gath[b + pad, 0], keys, (((1,), (1,)), ((), ())), preferred_element_type=jnp.float32
         )
         query_pos = b * rows + head_row
         first = jnp.zeros_like(query_pos)
@@ -433,18 +477,26 @@
                 obuf.at[b], attn_out.at[:, head_columns(me)], sem_o_recv.at[me]
             ).start()
 
-    @pl.loop(0, span)
-    def _(b):
-        wait_head(b)
-
-    @pl.loop(0, span)
-    def _(b):
+    own_heads.wait()
+
+    @pl.loop(1, span)
+    def _(k):
+        source = lax.rem(me + k, n)
+        send_head(source, source).wait_recv()
+
+    @pl.loop(0, n)
+    def _(i):
+        b = lax.rem(me + span + i, n)
+
+        @pl.when(i < n - span)
+        def _():
+            send_head(b, b).wait_recv()
+
         attend_block(b)
 
-    @pl.loop(span, n)
-    def _(b):
-        wait_head(b)
-        attend_block(b)
+    @pl.loop(first_tiles, tiles)
+    def _(i):
+        near_tile(i)
 
     own_state[...] = jnp.zeros(own_state.shape, jnp.float32)
     for earlier in range(planes):
@@ -469,7 +521,7 @@
         far = jnp.dot(
             far_powers[:, at], carried, precision=precise, preferred_element_type=jnp.float32
         )
-        hyena_out[:, at] = (query[:, at] * (near[:, at] + far)).astype(jnp.bfloat16)
+        hyena_out[:, at] = (feature_at(0, at) * (near[:, at] + far)).astype(jnp.bfloat16)
 
     @pl.when(me < n - 1)
     def _():
@@ -512,14 +564,20 @@
     return pl.pallas_call(
         functools.partial(fused_kernel, n),
         out_shape=(out, out),
-        in_specs=[vmem] * 4
-        + [pl.BlockSpec(memory_space=pltpu.SMEM), pl.BlockSpec(memory_space=pl.ANY)],
+        in_specs=[pl.BlockSpec(memory_space=pltpu.HBM)] * 6,
         out_specs=(vmem, vmem),
         scratch_shapes=[
-            pltpu.VMEM((n, streams, rows, HEAD), bf16),
+            pltpu.VMEM((streams, rows, channels), bf16),
+            pltpu.VMEM(short_weight.shape, f32),
+            pltpu.VMEM(filter_rate.T.shape, f32),
+            pltpu.VMEM(filter_rate.T.shape, f32),
+            pltpu.SMEM(doc_lengths.shape, jnp.int32),
+            pltpu.VMEM((n + min(SPAN, n) - 1, streams, rows, HEAD), bf16),
             pltpu.VMEM((n, rows, HEAD), bf16),
             pltpu.VMEM((streams, EDGE, channels), bf16),
-            pltpu.VMEM((rows, channels), f32),
+            pltpu.VMEM((rows, channels), bf16),
+            pltpu.VMEM((8, channels), f32),
+            pltpu.VMEM((8, channels), f32),
             pltpu.VMEM((rows, channels), f32),
             pltpu.VMEM((rows, channels), f32),
             pltpu.VMEM((modes, channels), f32),
@@ -537,6 +595,7 @@
             dma((PLANE,)),
             dma((n // PLANE,)),
             dma((n // PLANE,)),
+            dma((5,)),
         ],
         compiler_params=pltpu.CompilerParams(
             collective_id=0, has_side_effects=True, vmem_limit_bytes=48 * 2**20

time: 72.3 us -> 67.6 us (0.935)
  the two profiles are of different devices: /device:TPU:29 before, /device:TPU:0 now
where the time goes in v2:
time: 67.6 us; the launch traced here: 67.3 us
  Pallas kernels  59.3 us (88%)
  local copies, waits for them, and re-layouts  7.34 us (11%)
    pallas_call x1, Pallas kernels, by_heads(): pl.pallas_call(functools.partial(fused_kernel, n), out_shape=(out, out),...  59.3 us
    unnamed x14, local copies, waits for them, and re-layouts  7.34 us

profile of v2, /device:TPU:0, one launch (start us, length us, event | category | flops | bytes accessed | tf_op | source)
XLA Modules:
  0.0 67.3 jit_solution(12133366525148093716)
XLA Ops:
  0.6 0.0 copy-start
  0.6 1.4 %copy-done = bf16[128,3,2048]{2,0,1:T(8,128)(2,1)S(1)} copy-done((bf16[128,3,2048]{2,0,1:T(8,128)(2,1)S(1)}, bf16[128,3,2048]{2,0,1:T(8,128)(2,1)}, u32[]{:S(2)}) %copy-start) | copy-done | bytes 1572888
  2.0 0.0 copy-start.1
  2.0 1.4 %copy-done.1 = bf16[128,3,2048]{2,0,1:T(8,128)(2,1)S(1)} copy-done((bf16[128,3,2048]{2,0,1:T(8,128)(2,1)S(1)}, bf16[128,3,2048]{2,0,1:T(8,128)(2,1)}, u32[]{:S(2)}) %copy-start.1) | copy-done | bytes 1572888
  3.4 0.0 copy-start.2
  3.5 0.9 %copy-done.2 = f32[3,3,2048]{2,1,0:T(4,128)S(1)} copy-done((f32[3,3,2048]{2,1,0:T(4,128)S(1)}, f32[3,3,2048]{2,1,0:T(4,128)}, u32[]{:S(2)}) %copy-start.2) | copy-done | bytes 73752
  4.3 0.0 copy-start.3
  4.3 0.7 %copy-done.3 = f32[128,16]{0,1:T(8,128)S(1)} copy-done((f32[128,16]{0,1:T(8,128)S(1)}, f32[128,16]{0,1:T(8,128)}, u32[]{:S(2)}) %copy-start.3) | copy-done | bytes 8216
  5.0 0.0 copy-start.4
  5.0 0.7 %copy-done.4 = f32[128,16]{0,1:T(8,128)S(1)} copy-done((f32[128,16]{0,1:T(8,128)S(1)}, f32[128,16]{0,1:T(8,128)}, u32[]{:S(2)}) %copy-start.4) | copy-done | bytes 8216
  5.7 0.0 copy-start.5
  5.7 0.7 copy-done.5
  6.4 59.3 %shard_map.77 = (bf16[128,2048]{1,0:T(8,128)(2,1)S(1)}, bf16[128,2048]{1,0:T(8,128)(2,1)S(1)}) custom-call(bf16[3,128,2048]{2,1,0:T(8,128)(2,1)S(1)} %bitcast.4, f32[3,3,2048]{2,1,0:T(4,128)S(1)} %copy-done.2, f32[16,128]{1,0:T(8,128)S(1)} %bitcast.6, f32[16,128]{1,0:T(8,128)S(1)} %bitcast.7, s32[4]{0:T(128)S(1)} %copy-done.5, bf16[3,128,2048]{2,1,0:T(8,128)(2,1)S(1)} %bitcast.5), custom_call_target="tpu_custom_call" | custom-call | tf_op jit(solution)/shard_map/pallas_call | solution.py:564
  65.7 0.8 %copy.10 = bf16[128,2048]{1,0:T(8,128)(2,1)} copy(bf16[128,2048]{1,0:T(8,128)(2,1)S(1)} %get-tuple-element.4) | data formatting | bytes 1048576
  66.5 0.8 %copy.11 = bf16[128,2048]{1,0:T(8,128)(2,1)} copy(bf16[128,2048]{1,0:T(8,128)(2,1)S(1)} %get-tuple-element.5) | data formatting | bytes 1048576
Async XLA Ops:
  0.6 1.4 %copy-start = (bf16[128,3,2048]{2,0,1:T(8,128)(2,1)S(1)}, bf16[128,3,2048]{2,0,1:T(8,128)(2,1)}, u32[]{:S(2)}) copy-start(bf16[128,3,2048]{2,0,1:T(8,128)(2,1)} %param.6) | copy-start | bytes 4718596
  2.0 1.4 %copy-start.1 = (bf16[128,3,2048]{2,0,1:T(8,128)(2,1)S(1)}, bf16[128,3,2048]{2,0,1:T(8,128)(2,1)}, u32[]{:S(2)}) copy-start(bf16[128,3,2048]{2,0,1:T(8,128)(2,1)} %param.10) | copy-start | bytes 4718596
  3.4 0.9 %copy-start.2 = (f32[3,3,2048]{2,1,0:T(4,128)S(1)}, f32[3,3,2048]{2,1,0:T(4,128)}, u32[]{:S(2)}) copy-start(f32[3,3,2048]{2,1,0:T(4,128)} %short_hbm.1) | copy-start | bytes 221188
  4.3 0.7 %copy-start.3 = (f32[128,16]{0,1:T(8,128)S(1)}, f32[128,16]{0,1:T(8,128)}, u32[]{:S(2)}) copy-start(f32[128,16]{0,1:T(8,128)} %param.8) | copy-start | bytes 24580
  5.0 0.7 %copy-start.4 = (f32[128,16]{0,1:T(8,128)S(1)}, f32[128,16]{0,1:T(8,128)}, u32[]{:S(2)}) copy-start(f32[128,16]{0,1:T(8,128)} %param.9) | copy-start | bytes 24580
  5.7 0.7 copy-start.5
